TPU v7x, 32 devices: a whole 2x2x4 slice. The times are simulated.
32 devices in a mesh: grp: 2 (over y), clu: 4 (over z), arc: 4 (over x, core).
Axes of the slice: x: 2, y: 2, z: 4, core: 2. Of those that a mesh axis runs over, the one named last changes fastest.
Arguments:
- features: bfloat16 [8, 4, 16, 64, 128], P(('grp', 'clu'), 'arc'), parts along dimension 0, may hold values from -12 to 12
- cotangent: bfloat16 [8, 4, 16, 64, 128], P(('grp', 'clu'), 'arc'), parts along dimension 0, may hold values from -6 to 6
- w_out_att: bfloat16 [128, 384], replicated, may hold values from -0.5 to 0.5
- w_in_att: bfloat16 [128, 384], replicated, may hold values from -0.5 to 0.5
- w_mix: bfloat16 [256, 128], replicated, may hold values from -0.375 to 0.375
- in_degree: int32 [8, 4, 16], P(('grp', 'clu'), 'arc'), parts along dimension 0, may hold values from 1 to 128, 1024 in all within a row
- in_order: int32 [8, 4, 1024], P(('grp', 'clu'), 'arc'), parts along dimension 0, may hold values from 0 to 1023, each once within a row
Outputs:
- mixed: bfloat16 [8, 4, 16, 64, 128], P(('grp', 'clu'), 'arc'), parts along dimension 0
- feature_grad: bfloat16 [8, 4, 16, 64, 128], P(('grp', 'clu'), 'arc'), parts along dimension 0
There are 2 independent parts, one for each index of `grp`. A program takes and returns all parts, laid end to end along the dimension named above; an argument that names none is the same for every part. Nothing has to cross between parts.
Inputs may be any that keep to these rules, and one draw needn't show every extreme that they name: `in_degree`: the in-degrees of each block's 16 cities sum to 1024; some city of every block has exactly 128. `in_order`: each block's row holds every number below 1024 once.
All inputs are finite; a program needn't handle non-finite values.
Results may differ from a plain program's by a relative error of at most 0.014.
The roundings to bfloat16 on the way count: a program that leaves them out, or rounds other values in their place, can miss the bound.
Values may be sent and summed in bfloat16 or wider, within the bound.
A program may use at most 64 MiB of HBM per device.

v0:
```python
import math

import jax
import jax.numpy as jnp
from jax import lax
from jax.sharding import PartitionSpec as P

HEADS = 8
K = 64
CROSS = 16
IN_MAX = 128


def shifted(value, axis, steps):
    count = lax.axis_size(axis)
    pairs = [(source, (source + steps) % count) for source in range(count)]
    return lax.ppermute(value, axis, pairs)


def split_heads(tensor):
    return tensor.reshape(tensor.shape[:-1] + (HEADS, tensor.shape[-1] // HEADS))


def attend(projected, live_slots):
    feature_width = projected.shape[-1] // 3
    queries = split_heads(projected[..., :feature_width])
    key_rows = split_heads(projected[..., feature_width : 2 * feature_width])
    values = split_heads(projected[..., 2 * feature_width :])
    scores = jnp.einsum("bqhd,bkhd->bhqk", queries, key_rows, preferred_element_type=jnp.float32)
    scores = scores * (1.0 / math.sqrt(feature_width // HEADS))
    if live_slots is not None:
        scores = jnp.where(live_slots[:, None, None, :], scores, -1e30)
    highest = jnp.max(scores, axis=-1, keepdims=True)
    raised = jnp.exp(scores - highest)
    weights = (raised / jnp.sum(raised, axis=-1, keepdims=True)).astype(jnp.bfloat16)
    blended = jnp.einsum("bhqk,bkhd->bqhd", weights, values, preferred_element_type=jnp.float32)
    return blended.reshape(projected.shape[:-1] + (feature_width,)).astype(jnp.bfloat16)


def to_targets(field):
    peer_count = lax.axis_size("arc")
    inner = K - CROSS
    per_peer = inner // peer_count
    city_count = field.shape[0]
    channels = field.shape[-1]
    inside = field[:, :inner].reshape(city_count, peer_count, per_peer, channels)
    arrived = lax.all_to_all(inside, "arc", split_axis=1, concat_axis=1, tiled=True)
    onward = shifted(field[:, inner:], "clu", 1)
    return jnp.concatenate([arrived.reshape(-1, channels), onward.reshape(-1, channels)], axis=0)


def to_sources(grouped_rows):
    peer_count = lax.axis_size("arc")
    inner = K - CROSS
    per_peer = inner // peer_count
    channels = grouped_rows.shape[-1]
    city_count = grouped_rows.shape[0] // K
    inside = grouped_rows[: city_count * inner].reshape(city_count, peer_count, per_peer, channels)
    returned = lax.all_to_all(inside, "arc", split_axis=1, concat_axis=1, tiled=True).reshape(
        city_count, inner, channels
    )
    onward = grouped_rows[city_count * inner :].reshape(city_count, CROSS, channels)
    onward = shifted(onward, "clu", -1)
    return jnp.concatenate([returned, onward], axis=1)


def target_layout(degree, row_count):
    offsets = jnp.cumsum(degree) - degree
    slot_ids = jnp.arange(IN_MAX, dtype=jnp.int32)
    slot_index = jnp.minimum(offsets[:, None] + slot_ids[None, :], row_count - 1)
    live_slots = slot_ids[None, :] < degree[:, None]
    positions = jnp.arange(row_count, dtype=jnp.int32)
    started = offsets[None, :] <= positions[:, None]
    owner_ids = jnp.sum(started.astype(jnp.int32), axis=1) - 1
    starts = jnp.max(jnp.where(started, offsets[None, :], 0), axis=1)
    flat_index = owner_ids * IN_MAX + positions - starts
    return (slot_index, live_slots, flat_index)


def in_forward(tile_rows, live_slots, flat_index):
    blocks = tile_rows.reshape(-1, 8, IN_MAX, tile_rows.shape[-1])
    live_blocks = live_slots.reshape(-1, 8, IN_MAX)
    outcome = lax.map(lambda bundle: attend(bundle[0], bundle[1]), (blocks, live_blocks))
    return outcome.reshape(-1, outcome.shape[-1])[flat_index]


def in_backward(tile_rows, live_slots, slot_index, flat_index, d_grouped):
    d_tiles = jnp.where(live_slots[..., None], d_grouped[slot_index], jnp.zeros((), jnp.bfloat16))
    channels = tile_rows.shape[-1]
    blocks = tile_rows.reshape(-1, 8, IN_MAX, channels)
    live_blocks = live_slots.reshape(-1, 8, IN_MAX)
    grad_blocks = d_tiles.reshape(-1, 8, IN_MAX, d_tiles.shape[-1])

    def pull_block(bundle):
        _, pull = jax.vjp(lambda operand: attend(operand, bundle[1]), bundle[0])
        return pull(bundle[2])[0]

    grads = lax.map(pull_block, (blocks, live_blocks, grad_blocks))
    return grads.reshape(-1, channels)[flat_index]


def body(features, cotangent, w_out_att, w_in_att, w_mix, in_degree, in_order):
    city_count, arc_count, feature_width = features.shape[2:]
    row_count = city_count * arc_count
    home_rows = features.reshape(row_count, feature_width)
    upstream = cotangent.reshape(row_count, feature_width)
    degree = in_degree.reshape(city_count)
    target_order = in_order.reshape(row_count)
    inverse = (
        jnp.zeros((row_count,), jnp.int32)
        .at[target_order]
        .set(jnp.arange(row_count, dtype=jnp.int32))
    )
    slot_index, live_slots, flat_index = target_layout(degree, row_count)
    mix_grad = jnp.dot(upstream, w_mix.T, preferred_element_type=jnp.float32).astype(jnp.bfloat16)
    d_out = mix_grad[:, :feature_width].reshape(city_count, arc_count, feature_width)
    d_in = mix_grad[:, feature_width:].reshape(city_count, arc_count, feature_width)
    outgoing = home_rows.reshape(city_count, arc_count, feature_width)
    arrived = to_targets(outgoing)[target_order]
    d_in_grouped = None
    grouped = jnp.dot(arrived, w_in_att, preferred_element_type=jnp.float32).astype(jnp.bfloat16)
    proj_out = jnp.dot(home_rows, w_out_att, preferred_element_type=jnp.float32).astype(
        jnp.bfloat16
    )
    proj_out = proj_out.reshape(city_count, arc_count, 3 * feature_width)
    tile_rows = grouped[slot_index]
    in_grouped = in_forward(tile_rows, live_slots, flat_index)
    out_att = attend(proj_out, None)
    d_in_grouped = to_targets(d_in)[target_order]
    _, out_pull = jax.vjp(lambda operand: attend(operand, None), proj_out)
    d_proj_out = out_pull(d_out)[0]
    d_grouped = in_backward(tile_rows, live_slots, slot_index, flat_index, d_in_grouped)
    back_rows = jnp.dot(d_grouped, w_in_att.T, preferred_element_type=jnp.float32).astype(
        jnp.bfloat16
    )
    in_att = to_sources(in_grouped[inverse])
    returned = to_sources(back_rows[inverse])
    in_grad = returned.reshape(row_count, feature_width)
    combined = jnp.concatenate(
        [out_att.reshape(row_count, feature_width), in_att.reshape(row_count, feature_width)],
        axis=1,
    )
    mixed = (
        home_rows.astype(jnp.float32) + jnp.dot(combined, w_mix, preferred_element_type=jnp.float32)
    ).astype(jnp.bfloat16)
    out_grad = jnp.dot(
        d_proj_out.reshape(row_count, 3 * feature_width),
        w_out_att.T,
        preferred_element_type=jnp.float32,
    )
    feature_grad = (upstream.astype(jnp.float32) + out_grad + in_grad.astype(jnp.float32)).astype(
        jnp.bfloat16
    )
    return (mixed.reshape(features.shape), feature_grad.reshape(features.shape))


def solution(mesh):
    in_specs = (
        P(("grp", "clu"), "arc", None, None, None),
        P(("grp", "clu"), "arc", None, None, None),
        P(),
        P(),
        P(),
        P(("grp", "clu"), "arc", None),
        P(("grp", "clu"), "arc", None),
    )
    out_specs = (
        P(("grp", "clu"), "arc", None, None, None),
        P(("grp", "clu"), "arc", None, None, None),
    )
    return jax.shard_map(body, mesh=mesh, in_specs=in_specs, out_specs=out_specs, check_vma=False)
```

profile of v0, /device:TPU:0, one launch (start us, length us, event | category | flops | bytes accessed | tf_op | source)
XLA Modules:
  0.0 146.5 jit_solution(1695397000991884692)
XLA Ops:
  0.7 1.2 copy.193
  2.5 4.2 %all-to-all-start = ((bf16[16,4,12,128]{3,0,2,1:T(8,128)(2,1)}), bf16[16,4,12,128]{3,0,2,1:T(8,128)(2,1)S(1)}, u32[]{:S(2)}, u32[]{:S(2)}) async-start(bf16[16,4,12,128]{3,0,2,1:T(8,128)(2,1)} %bitcast.29), calls=%async_computation | async-start | bytes 393216 | tf_op jit(solution)/shard_map/all_to_all | solution.py:47
  6.7 2.2 %collective-permute-start = (bf16[16,16,128]{2,0,1:T(8,128)(2,1)S(1)}, bf16[16,16,128]{2,0,1:T(8,128)(2,1)S(1)}, u32[]{:S(2)}, u32[]{:S(2)}) collective-permute-start(bf16[16,16,128]{2,0,1:T(8,128)(2,1)S(1)} %slice.99), channel_id=1, source_target_pairs={{0,4},{4,8},{8,12},{12,0},{1,5},{5,9},{9,13},{13,1},{2,6},{6,10},{... | collective-permute-start | bytes 196616 | tf_op jit(solution)/shard_map/ppermute | solution.py:17
  9.0 1.2 convolution_convert_fusion.6
  10.3 1.6 %collective-permute-start.2 = (bf16[16,16,128]{2,1,0:T(8,128)(2,1)S(1)}, bf16[16,16,128]{2,1,0:T(8,128)(2,1)}, u32[]{:S(2)}, u32[]{:S(2)}) collective-permute-start(bf16[16,16,128]{2,1,0:T(8,128)(2,1)S(1)} %slice.105), channel_id=1, source_target_pairs={{0,4},{4,8},{8,12},{12,0},{1,5},{5,9},{9,13},{13,1},{2,6},{6,10},{... | collective-permute-start | bytes 196616 | tf_op jit(solution)/shard_map/ppermute | solution.py:17
  16.6 1.2 fusion.50
  17.8 2.9 %convert_reduce_fusion.1 = (f32[16,8,64]{2,1,0:T(8,128)S(1)}, pred[16,8,64,64]{2,3,1,0:T(32,128)(4,1)S(1)}, f32[16,8,64]{2,1,0:T(8,128)S(1)}, bf16[16,8,64,64]{2,3,1,0:T(8,128)(2,1)S(1)}) fusion(f32[16,8,64]{2,1,0:T(8,128)S(1)} %get-tuple-element.145, f32[16,8,64,64]{2,3,1,0:T(8,128)S(1)} %get-tuple-element.146, ...), kind=kOutput, calls=%fused_computation.74 | convolution fusion | flops 22003712 | bytes 4325376 | tf_op jit(solution)/shard_map/transpose(jvp(bhqk,bkhd->bqhd))/dot_general | solution.py:36
  20.8 2.1 %fusion.76 = (f32[16,8,64]{2,1,0:T(8,128)S(1)}, f32[16,8,64,64]{2,3,1,0:T(8,128)S(1)}, bf16[16,8,64,64]{2,3,1,0:T(8,128)(2,1)S(1)}) fusion(f32[16,8,64]{2,1,0:T(8,128)S(1)} %get-tuple-element.145, f32[16,8,64,64]{2,3,1,0:T(8,128)S(1)} %get-tuple-element.146, f32[16,8,64]{2,1,0:T(8,128)S(1)} %neg.18, f32[16,8,64]{2,1,0:T(8,128)S(1)} %fusion.50, ...), kind=kLoop, calls=%fused_computation.142 | loop fusion | flops 4710400 | bytes 6422528 | tf_op jit(solution)/shard_map/transpose(jvp())/reduce_sum | solution.py:34
  23.8 1.2 fusion.51
  25.1 1.2 convolution_convert_fusion.4
  26.3 1.5 %fusion.53 = bf16[16,64,8,16]{1,3,2,0:T(8,128)(2,1)} fusion(bf16[16,64,8,16]{1,3,2,0:T(8,128)(2,1)S(1)} %bitcast.209, bf16[16,8,64,64]{2,3,1,0:T(8,128)(2,1)S(1)} %get-tuple-element.138), kind=kOutput, calls=%fused_computation.96 | convolution fusion | flops 16908288 | bytes 1572864 | tf_op jit(solution)/shard_map/bhqk,bkhd->bqhd/dot_general | solution.py:36
  29.0 4.5 %scatter_custom_fusion = s32[1024]{0:T(1024)S(1)} fusion(s32[1024]{0:T(1024)S(1)} %bitcast.229, s32[1024]{0:T(1024)S(1)} %iota.25, s32[]{:T(128)} %copy.218), kind=kCustom, calls=%fused_computation.133 | custom fusion | bytes 4100 | tf_op jit(solution)/shard_map/scatter | solution.py:112
  37.2 3.4 %all-to-all-start.2 = ((bf16[16,4,12,128]{3,0,2,1:T(8,128)(2,1)}), bf16[16,4,12,128]{3,0,2,1:T(8,128)(2,1)S(1)}, u32[]{:S(2)}, u32[]{:S(2)}) async-start(bf16[16,4,12,128]{3,0,2,1:T(8,128)(2,1)} %bitcast.55), calls=%async_computation.2 | async-start | bytes 393216 | tf_op jit(solution)/shard_map/all_to_all | solution.py:47
  40.7 3.2 %gather_fusion = bf16[1024,128]{1,0:T(8,128)(2,1)S(1)} fusion(bf16[1024,128]{1,0:T(8,128)(2,1)S(1)} %pad_maximum_fusion, s32[1024]{0:T(1024)S(1)} %broadcast_clamp_fusion.1), kind=kCustom, calls=%fused_computation | custom fusion | bytes 528384 | tf_op jit(solution)/shard_map/gather | solution.py:119
  44.3 9.1 %gather_fusion.1 = bf16[2048,384]{1,0:T(8,128)(2,1)} fusion(bf16[1024,384]{1,0:T(8,128)(2,1)S(1)} %convolution_convert_fusion.2, s32[2048]{0:T(1024)S(1)} %fusion.64), kind=kCustom, calls=%fused_computation.1 | custom fusion | bytes 3153920 | tf_op jit(solution)/shard_map/gather | solution.py:126
  53.4 1.9 %copy.144 = bf16[2,8,128,384]{2,3,1,0:T(8,128)(2,1)S(1)} copy(bf16[2,8,128,384]{3,2,1,0:T(8,128)(2,1)} %bitcast.198) | data formatting | bytes 3145728 | tf_op jit(solution)/shard_map/while | solution.py:83
  55.3 14.0 %while.20 = (s32[]{:T(128)}, bf16[2,8,128,128]{3,2,1,0:T(8,128)(2,1)S(1)}, bf16[2,8,128,384]{2,3,1,0:T(8,128)(2,1)S(1)}, pred[2,8,128]{2,1,0:T(8,128)(4,1)S(1)}, s32[]{:T(128)}) while((s32[]{:T(128)}, bf16[2,8,128,128]{3,2,1,0:T(8,128)(2,1)S(1)}, bf16[2,8,128,384]{2,3,1,0:T(8,128)(2,1)S(1)}, pred[2,8,128]{2,1,0:T(8,128)(4,1)S(1)}, ...), condition=%wide.region_6.7_spmd, body=%wide.region_3.6_spmd.sunk | while | flops 73531520 | bytes 13700177 | solution.py:83
  55.4 3.7 %fusion.138 = (f32[8,8,128]{2,1,0:T(8,128)S(1)}, f32[8,8,128,128]{2,3,1,0:T(8,128)}) fusion(pred[8,128]{1,0:T(8,128)(4,1)S(1)} %dynamic-slice_bitcast_fusion.9, bf16[8,128,8,16]{1,3,2,0:T(8,128)(2,1)S(1)} %bitcast.196, bf16[8,128,8,16]{1,3,2,0:T(8,128)(2,1)S(1)} %bitcast.195), kind=kOutput, calls=%fused_computation.144.clone.1 | convolution fusion | flops 37748864 | bytes 4752384 | tf_op jit(solution)/shard_map/while/body/eval_jaxpr/sub | solution.py:34
  59.2 2.8 %fusion.139 = bf16[8,8,16,128]{3,2,1,0:T(8,128)(2,1)S(1)} fusion(bf16[8,128,8,16]{1,3,2,0:T(8,128)(2,1)S(1)} %bitcast.193, f32[8,8,128,128]{2,3,1,0:T(8,128)} %get-tuple-element.218, f32[8,8,128]{2,1,0:T(8,128)S(1)} %get-tuple-element.219), kind=kOutput, calls=%fused_computation.18.clone.1 | convolution fusion | flops 35782656 | bytes 4751360 | tf_op jit(solution)/shard_map/while/body/eval_jaxpr/bhqk,bkhd->bqhd/dot_general | solution.py:36
  62.4 3.7 %fusion.138 = (f32[8,8,128]{2,1,0:T(8,128)S(1)}, f32[8,8,128,128]{2,3,1,0:T(8,128)}) fusion(pred[8,128]{1,0:T(8,128)(4,1)S(1)} %dynamic-slice_bitcast_fusion.9, bf16[8,128,8,16]{1,3,2,0:T(8,128)(2,1)S(1)} %bitcast.196, bf16[8,128,8,16]{1,3,2,0:T(8,128)(2,1)S(1)} %bitcast.195), kind=kOutput, calls=%fused_computation.144.clone.1 | convolution fusion | flops 37748864 | bytes 4752384 | tf_op jit(solution)/shard_map/while/body/eval_jaxpr/sub | solution.py:34
  66.1 2.8 %fusion.139 = bf16[8,8,16,128]{3,2,1,0:T(8,128)(2,1)S(1)} fusion(bf16[8,128,8,16]{1,3,2,0:T(8,128)(2,1)S(1)} %bitcast.193, f32[8,8,128,128]{2,3,1,0:T(8,128)} %get-tuple-element.218, f32[8,8,128]{2,1,0:T(8,128)S(1)} %get-tuple-element.219), kind=kOutput, calls=%fused_computation.18.clone.1 | convolution fusion | flops 35782656 | bytes 4751360 | tf_op jit(solution)/shard_map/while/body/eval_jaxpr/bhqk,bkhd->bqhd/dot_general | solution.py:36
  69.2 3.2 %gather_fusion.2 = bf16[1024,128]{1,0:T(8,128)(2,1)S(1)} fusion(bf16[2048,128]{1,0:T(8,128)(2,1)S(1)} %bitcast.187, s32[1024]{0:T(1024)S(1)} %broadcast_clamp_fusion), kind=kCustom, calls=%fused_computation.2 | custom fusion | bytes 528384 | tf_op jit(solution)/shard_map/gather | solution.py:84
  72.5 3.2 %gather_fusion.3 = bf16[1024,128]{1,0:T(8,128)(2,1)S(1)} fusion(bf16[1024,128]{1,0:T(8,128)(2,1)S(1)} %gather_fusion.2, s32[1024]{0:T(1024)S(1)} %fusion.65), kind=kCustom, calls=%fused_computation.3 | custom fusion | bytes 528384 | tf_op jit(solution)/shard_map/gather | solution.py:136
  76.7 3.2 %gather_fusion.4 = bf16[1024,128]{1,0:T(8,128)(2,1)S(1)} fusion(bf16[1024,128]{1,0:T(8,128)(2,1)S(1)} %pad_maximum_fusion.2, s32[1024]{0:T(1024)S(1)} %broadcast_clamp_fusion.1), kind=kCustom, calls=%fused_computation.4 | custom fusion | bytes 528384 | tf_op jit(solution)/shard_map/gather | solution.py:129
  79.9 6.2 %gather_fusion.5 = bf16[2048,128]{1,0:T(8,128)(2,1)S(1)} fusion(bf16[1024,128]{1,0:T(8,128)(2,1)S(1)} %gather_fusion.4, s32[2048]{0:T(1024)S(1)} %fusion.64), kind=kCustom, calls=%fused_computation.5 | custom fusion | bytes 1056768 | tf_op jit(solution)/shard_map/gather | solution.py:88
  88.8 3.4 %all-to-all-start.1 = ((bf16[16,4,12,128]{3,0,2,1:T(8,128)(2,1)}), bf16[16,4,12,128]{3,0,2,1:T(8,128)(2,1)S(1)}, u32[]{:S(2)}, u32[]{:S(2)}) async-start(bf16[16,4,12,128]{3,0,2,1:T(8,128)(2,1)} %copy.146), calls=%async_computation.1 | async-start | bytes 393216 | tf_op jit(solution)/shard_map/all_to_all | solution.py:59
  92.1 2.3 %collective-permute-start.1 = (bf16[16,16,128]{2,0,1:T(8,128)(2,1)}, bf16[16,16,128]{2,0,1:T(8,128)(2,1)}, u32[]{:S(2)}, u32[]{:S(2)}) collective-permute-start(bf16[16,16,128]{2,0,1:T(8,128)(2,1)} %copy.147), channel_id=1, source_target_pairs={{0,12},{4,0},{8,4},{12,8},{1,13},{5,1},{9,5},{13,9},{2,14},{6,2},{... | collective-permute-start | bytes 196616 | tf_op jit(solution)/shard_map/ppermute | solution.py:17
  94.4 28.6 %while.21 = (s32[]{:T(128)}, bf16[2,8,128,384]{3,2,1,0:T(8,128)(2,1)}, bf16[2,8,128,128]{2,3,1,0:T(8,128)(2,1)}, pred[2,8,128]{2,1,0:T(8,128)(4,1)S(1)}, bf16[2,8,128,384]{2,3,1,0:T(8,128)(2,1)S(1)}, /*index=5*/s32[]{:T(128)}) while((s32[]{:T(128)}, bf16[2,8,128,384]{3,2,1,0:T(8,128)(2,1)}, bf16[2,8,128,128]{2,3,1,0:T(8,128)(2,1)}, ...), condition=%wide.region_19.20_spmd, body=%wide.region_13.19_spmd.sunk | while | flops 211419136 | bytes 52634716 | solution.py:98
  95.5 1.3 fusion.148
  96.8 1.3 fusion.149
  98.1 1.8 %fusion.153 = bf16[8,8,16,128]{3,2,1,0:T(8,128)(2,1)S(1)} fusion(bf16[8,8,16,128]{3,2,1,0:T(8,128)(2,1)S(1)} %bitcast.188, f32[8,8,128]{2,1,0:T(8,128)S(1)} %fusion.149, f32[8,8,128,128]{2,3,1,0:T(8,128)S(1)} %get-tuple-element.228, f32[8,8,128]{2,1,0:T(8,128)S(1)} %get-tuple-element.227, pred[8,128]{1,0:T(8,128)(4,1)S(1)} %dynamic-slice_bitcast_fusion.11), kind=kOutput, calls=%fused_computation.52.clone.1 | convolution fusion | flops 38928384 | bytes 4785152 | tf_op jit(solution)/shard_map/while/body/eval_jaxpr/transpose(jvp(bhqk,bkhd->bqhd))/dot_general | solution.py:36
  99.9 3.0 %convert_reduce_fusion.4 = (f32[8,8,128]{2,1,0:T(8,128)S(1)}, pred[8,8,128,128]{2,3,1,0:T(32,128)(4,1)S(1)}, f32[8,8,128]{2,1,0:T(8,128)S(1)}, bf16[8,8,128,128]{2,3,1,0:T(8,128)(2,1)S(1)}) fusion(f32[8,8,128]{2,1,0:T(8,128)S(1)} %get-tuple-element.227, f32[8,8,128,128]{2,3,1,0:T(8,128)S(1)} %get-tuple-element.228, ...), kind=kOutput, calls=%fused_computation.32.clone.1 | convolution fusion | flops 45072384 | bytes 7996416 | tf_op jit(solution)/shard_map/while/body/eval_jaxpr/transpose(jvp(bhqk,bkhd->bqhd))/dot_general | solution.py:36
  102.9 2.0 %fusion.150 = (f32[8,8,128]{2,1,0:T(8,128)S(1)}, f32[8,8,128,128]{2,3,1,0:T(8,128)S(1)}) fusion(f32[8,8,128]{2,1,0:T(8,128)S(1)} %get-tuple-element.227, f32[8,8,128,128]{2,3,1,0:T(8,128)S(1)} %get-tuple-element.228, pred[8,128]{1,0:T(8,128)(4,1)S(1)} %dynamic-slice_bitcast_fusion.11, f32[8,8,128]{2,1,0:T(8,128)S(1)} %neg.25, ...), kind=kLoop, calls=%fused_computation.141.clone.1 | loop fusion | flops 8380416 | bytes 10617856 | tf_op jit(solution)/shard_map/while/body/eval_jaxpr/transpose(jvp())/reduce_sum | solution.py:34
  105.0 1.3 fusion.152
  106.2 1.1 fusion.151
  109.8 1.3 fusion.148
  111.1 1.3 fusion.149
  112.4 1.8 %fusion.153 = bf16[8,8,16,128]{3,2,1,0:T(8,128)(2,1)S(1)} fusion(bf16[8,8,16,128]{3,2,1,0:T(8,128)(2,1)S(1)} %bitcast.188, f32[8,8,128]{2,1,0:T(8,128)S(1)} %fusion.149, f32[8,8,128,128]{2,3,1,0:T(8,128)S(1)} %get-tuple-element.228, f32[8,8,128]{2,1,0:T(8,128)S(1)} %get-tuple-element.227, pred[8,128]{1,0:T(8,128)(4,1)S(1)} %dynamic-slice_bitcast_fusion.11), kind=kOutput, calls=%fused_computation.52.clone.1 | convolution fusion | flops 38928384 | bytes 4785152 | tf_op jit(solution)/shard_map/while/body/eval_jaxpr/transpose(jvp(bhqk,bkhd->bqhd))/dot_general | solution.py:36
  114.2 3.0 %convert_reduce_fusion.4 = (f32[8,8,128]{2,1,0:T(8,128)S(1)}, pred[8,8,128,128]{2,3,1,0:T(32,128)(4,1)S(1)}, f32[8,8,128]{2,1,0:T(8,128)S(1)}, bf16[8,8,128,128]{2,3,1,0:T(8,128)(2,1)S(1)}) fusion(f32[8,8,128]{2,1,0:T(8,128)S(1)} %get-tuple-element.227, f32[8,8,128,128]{2,3,1,0:T(8,128)S(1)} %get-tuple-element.228, ...), kind=kOutput, calls=%fused_computation.32.clone.1 | convolution fusion | flops 45072384 | bytes 7996416 | tf_op jit(solution)/shard_map/while/body/eval_jaxpr/transpose(jvp(bhqk,bkhd->bqhd))/dot_general | solution.py:36
  117.2 2.0 %fusion.150 = (f32[8,8,128]{2,1,0:T(8,128)S(1)}, f32[8,8,128,128]{2,3,1,0:T(8,128)S(1)}) fusion(f32[8,8,128]{2,1,0:T(8,128)S(1)} %get-tuple-element.227, f32[8,8,128,128]{2,3,1,0:T(8,128)S(1)} %get-tuple-element.228, pred[8,128]{1,0:T(8,128)(4,1)S(1)} %dynamic-slice_bitcast_fusion.11, f32[8,8,128]{2,1,0:T(8,128)S(1)} %neg.25, ...), kind=kLoop, calls=%fused_computation.141.clone.1 | loop fusion | flops 8380416 | bytes 10617856 | tf_op jit(solution)/shard_map/while/body/eval_jaxpr/transpose(jvp())/reduce_sum | solution.py:34
  119.2 1.3 fusion.152
  120.5 1.1 fusion.151
  123.0 5.4 %gather_fusion.6 = bf16[1024,384]{1,0:T(8,128)(2,1)S(1)} fusion(bf16[2048,384]{1,0:T(8,128)(2,1)} %bitcast.186, s32[1024]{0:T(1024)S(1)} %broadcast_clamp_fusion), kind=kCustom, calls=%fused_computation.6 | custom fusion | bytes 1576960 | tf_op jit(solution)/shard_map/gather | solution.py:99
  128.9 3.2 %gather_fusion.7 = bf16[1024,128]{1,0:T(8,128)(2,1)S(1)} fusion(bf16[1024,128]{1,0:T(8,128)(2,1)S(1)} %convolution_convert_fusion.7, s32[1024]{0:T(1024)S(1)} %fusion.65), kind=kCustom, calls=%fused_computation.7 | custom fusion | bytes 528384 | tf_op jit(solution)/shard_map/gather | solution.py:137
  133.0 4.0 %all-to-all-start.3 = ((bf16[16,4,12,128]{3,0,2,1:T(8,128)(2,1)}), bf16[16,4,12,128]{3,0,2,1:T(8,128)(2,1)}, u32[]{:S(2)}, u32[]{:S(2)}) async-start(bf16[16,4,12,128]{3,0,2,1:T(8,128)(2,1)} %copy.163), calls=%async_computation.3 | async-start | bytes 393216 | tf_op jit(solution)/shard_map/all_to_all | solution.py:59
  139.3 3.1 %collective-permute-done.3 = bf16[16,16,128]{2,0,1:T(8,128)(2,1)S(1)} collective-permute-done((bf16[16,16,128]{2,0,1:T(8,128)(2,1)S(1)}, bf16[16,16,128]{2,0,1:T(8,128)(2,1)S(1)}, u32[]{:S(2)}, u32[]{:S(2)}) %collective-permute-start.3) | collective-permute-done | bytes 65568 | tf_op jit(solution)/shard_map/ppermute | solution.py:17
  143.5 1.9 %fusion.54 = bf16[1024,128]{1,0:T(8,128)(2,1)} fusion(bf16[256,128]{1,0:T(8,128)(2,1)} %param.15, bf16[1024,128]{0,1:T(8,128)(2,1)S(1)} %copy.149, bf16[1024,128]{0,1:T(8,128)(2,1)S(1)} %convert_element_type.130, bf16[1024,128]{1,0:T(8,128)(2,1)S(1)} %bitcast.215), kind=kOutput, calls=%fused_computation.99 | convolution fusion | flops 68550656 | bytes 1114112 | tf_op jit(solution)/shard_map/dot_general | solution.py:144
  145.4 1.1 fusion.58
  (131 shorter events, 25.6 us)
Async XLA Ops:
  0.6 43.3 %copy-start = (bf16[128,384]{1,0:T(8,128)(2,1)S(1)}, bf16[128,384]{1,0:T(8,128)(2,1)}, u32[]{:S(2)}) copy-start(bf16[128,384]{1,0:T(8,128)(2,1)} %param.14) | copy-start | bytes 294916
  0.6 13.5 %copy-start.5 = (bf16[1,1,16,64,128]{4,3,2,1,0:T(8,128)(2,1)S(1)}, bf16[1,1,16,64,128]{4,3,2,1,0:T(8,128)(2,1)}, u32[]{:S(2)}) copy-start(bf16[1,1,16,64,128]{4,3,2,1,0:T(8,128)(2,1)} %param.11) | copy-start | bytes 786436
  0.7 13.5 %copy-start.8 = (bf16[128,384]{1,0:T(8,128)(2,1)S(1)}, bf16[128,384]{1,0:T(8,128)(2,1)}, u32[]{:S(2)}) copy-start(bf16[128,384]{1,0:T(8,128)(2,1)} %param.13) | copy-start | bytes 294916
  2.5 34.6 %all-to-all-start = ((bf16[16,4,12,128]{3,0,2,1:T(8,128)(2,1)}), bf16[16,4,12,128]{3,0,2,1:T(8,128)(2,1)S(1)}, u32[]{:S(2)}, u32[]{:S(2)}) async-start(bf16[16,4,12,128]{3,0,2,1:T(8,128)(2,1)} %bitcast.29), calls=%async_computation | async-start | bytes 393216 | tf_op jit(solution)/shard_map/all_to_all | solution.py:47
  6.7 30.4 %collective-permute-start = (bf16[16,16,128]{2,0,1:T(8,128)(2,1)S(1)}, bf16[16,16,128]{2,0,1:T(8,128)(2,1)S(1)}, u32[]{:S(2)}, u32[]{:S(2)}) collective-permute-start(bf16[16,16,128]{2,0,1:T(8,128)(2,1)S(1)} %slice.99), channel_id=1, source_target_pairs={{0,4},{4,8},{8,12},{12,0},{1,5},{5,9},{9,13},{13,1},{2,6},{6,10},{... | collective-permute-start | bytes 196616 | tf_op jit(solution)/shard_map/ppermute | solution.py:17
  10.3 65.6 %collective-permute-start.2 = (bf16[16,16,128]{2,1,0:T(8,128)(2,1)S(1)}, bf16[16,16,128]{2,1,0:T(8,128)(2,1)}, u32[]{:S(2)}, u32[]{:S(2)}) collective-permute-start(bf16[16,16,128]{2,1,0:T(8,128)(2,1)S(1)} %slice.105), channel_id=1, source_target_pairs={{0,4},{4,8},{8,12},{12,0},{1,5},{5,9},{9,13},{13,1},{2,6},{6,10},{... | collective-permute-start | bytes 196616 | tf_op jit(solution)/shard_map/ppermute | solution.py:17
  25.0 3.2 %copy-start.11 = (s32[1,1,16]{2,1,0:T(1,128)S(1)}, s32[1,1,16]{2,1,0:T(1,128)}, u32[]{:S(2)}) copy-start(s32[1,1,16]{2,1,0:T(1,128)} %param.16) | copy-start | bytes 196
  25.1 4.0 %copy-start.10 = (s32[1,1,1024]{2,1,0:T(1,128)S(1)}, s32[1,1,1024]{2,1,0:T(1,128)}, u32[]{:S(2)}) copy-start(s32[1,1,1024]{2,1,0:T(1,128)} %param.17) | copy-start | bytes 12292
  37.2 38.5 %all-to-all-start.2 = ((bf16[16,4,12,128]{3,0,2,1:T(8,128)(2,1)}), bf16[16,4,12,128]{3,0,2,1:T(8,128)(2,1)S(1)}, u32[]{:S(2)}, u32[]{:S(2)}) async-start(bf16[16,4,12,128]{3,0,2,1:T(8,128)(2,1)} %bitcast.55), calls=%async_computation.2 | async-start | bytes 393216 | tf_op jit(solution)/shard_map/all_to_all | solution.py:47
  88.8 44.2 %all-to-all-start.1 = ((bf16[16,4,12,128]{3,0,2,1:T(8,128)(2,1)}), bf16[16,4,12,128]{3,0,2,1:T(8,128)(2,1)S(1)}, u32[]{:S(2)}, u32[]{:S(2)}) async-start(bf16[16,4,12,128]{3,0,2,1:T(8,128)(2,1)} %copy.146), calls=%async_computation.1 | async-start | bytes 393216 | tf_op jit(solution)/shard_map/all_to_all | solution.py:59
  92.1 46.0 %collective-permute-start.1 = (bf16[16,16,128]{2,0,1:T(8,128)(2,1)}, bf16[16,16,128]{2,0,1:T(8,128)(2,1)}, u32[]{:S(2)}, u32[]{:S(2)}) collective-permute-start(bf16[16,16,128]{2,0,1:T(8,128)(2,1)} %copy.147), channel_id=1, source_target_pairs={{0,12},{4,0},{8,4},{12,8},{1,13},{5,1},{9,5},{13,9},{2,14},{6,2},{... | collective-permute-start | bytes 196616 | tf_op jit(solution)/shard_map/ppermute | solution.py:17
  128.4 8.5 %copy-start.2 = (bf16[16,64,128]{2,1,0:T(8,128)(2,1)S(1)}, bf16[16,64,128]{2,1,0:T(8,128)(2,1)}, u32[]{:S(2)}) copy-start(bf16[16,64,128]{2,1,0:T(8,128)(2,1)} %copy.155) | copy-start | bytes 786436
  128.5 8.5 %copy-start.3 = (bf16[16,64,128]{2,1,0:T(8,128)(2,1)S(1)}, bf16[16,64,128]{2,1,0:T(8,128)(2,1)}, u32[]{:S(2)}) copy-start(bf16[16,64,128]{2,1,0:T(8,128)(2,1)} %copy.157) | copy-start | bytes 786436
  128.5 8.5 %copy-start.4 = (bf16[16,64,128]{2,1,0:T(8,128)(2,1)S(1)}, bf16[16,64,128]{2,1,0:T(8,128)(2,1)}, u32[]{:S(2)}) copy-start(bf16[16,64,128]{2,1,0:T(8,128)(2,1)} %copy.153) | copy-start | bytes 786436
  128.5 8.7 %copy-start.1 = (bf16[16,64,8,16]{1,3,2,0:T(8,128)(2,1)S(1)}, bf16[16,64,8,16]{1,3,2,0:T(8,128)(2,1)}, u32[]{:S(2)}) copy-start(bf16[16,64,8,16]{1,3,2,0:T(8,128)(2,1)} %fusion.53) | copy-start | bytes 786436
  132.1 11.4 %copy-start.6 = (bf16[1,1,16,64,128]{4,3,2,1,0:T(8,128)(2,1)S(1)}, bf16[1,1,16,64,128]{4,3,2,1,0:T(8,128)(2,1)}, u32[]{:S(2)}) copy-start(bf16[1,1,16,64,128]{4,3,2,1,0:T(8,128)(2,1)} %param.11) | copy-start | bytes 786436
  133.0 9.4 %all-to-all-start.3 = ((bf16[16,4,12,128]{3,0,2,1:T(8,128)(2,1)}), bf16[16,4,12,128]{3,0,2,1:T(8,128)(2,1)}, u32[]{:S(2)}, u32[]{:S(2)}) async-start(bf16[16,4,12,128]{3,0,2,1:T(8,128)(2,1)} %copy.163), calls=%async_computation.3 | async-start | bytes 393216 | tf_op jit(solution)/shard_map/all_to_all | solution.py:59
  137.0 8.4 %copy-start.7 = (bf16[1,1,16,64,128]{4,3,2,1,0:T(8,128)(2,1)S(1)}, bf16[1,1,16,64,128]{4,3,2,1,0:T(8,128)(2,1)}, u32[]{:S(2)}) copy-start(bf16[1,1,16,64,128]{4,3,2,1,0:T(8,128)(2,1)} %param.12) | copy-start | bytes 786436
  137.0 8.4 %copy-start.9 = (bf16[128,384]{1,0:T(8,128)(2,1)S(1)}, bf16[128,384]{1,0:T(8,128)(2,1)}, u32[]{:S(2)}) copy-start(bf16[128,384]{1,0:T(8,128)(2,1)} %param.13) | copy-start | bytes 294916
  137.9 4.5 %collective-permute-start.3 = (bf16[16,16,128]{2,0,1:T(8,128)(2,1)S(1)}, bf16[16,16,128]{2,0,1:T(8,128)(2,1)S(1)}, u32[]{:S(2)}, u32[]{:S(2)}) collective-permute-start(bf16[16,16,128]{2,0,1:T(8,128)(2,1)S(1)} %copy.164), channel_id=1, source_target_pairs={{0,12},{4,0},{8,4},{12,8},{1,13},{5,1},{9,5},{13,9},{2,14},{6,2},{... | collective-permute-start | bytes 196616 | tf_op jit(solution)/shard_map/ppermute | solution.py:17
where the time goes:
time: 147 us
  local copies, waits for them, and re-layouts  61 us (41%)
  matrix products  44 us (30%)
  starting transfers between devices  21.4 us (15%)
  other arithmetic  15.4 us (10%)
  waiting for transfers between devices  3.14 us (2%)
    dot_general x9, matrix products, attend(): jnp.einsum('bhqk,bkhd->bqhd', weights, values, preferred_element_type=jnp...  20.9 us
    dot_general x9, matrix products, attend(): jnp.einsum('bqhd,bkhd->bhqk', queries, key_rows, preferred_element_type=j...  10.3 us
    gather x1, local copies, waits for them, and re-layouts, body(): tile_rows = grouped[slot_index]  9.05 us
    all_to_all x2, starting transfers between devices, to_targets(): lax.all_to_all(inside, 'arc', split_axis=1, concat_axis=1, tiled=True)  7.58 us
    sub x2, matrix products, attend(): raised = jnp.exp(scores - highest)  7.47 us
    all_to_all x2, starting transfers between devices, to_sources(): lax.all_to_all(inside, 'arc', split_axis=1, concat_axis=1, tiled=True)  7.36 us
    gather x2, local copies, waits for them, and re-layouts, in_backward(): d_grouped[slot_index]  6.47 us
    ppermute x4, starting transfers between devices, shifted(): return lax.ppermute(value, axis, pairs)  6.46 us
  transfers between devices with their start and end apart: 8, of which 1 were waited for; matrix products, arithmetic and copies ran while one was open for 69% of the time, Pallas kernels for 0%

commit v1 on v0

v1 whole, which is shorter than its diff:
```python
import functools

import jax
import jax.numpy as jnp
from jax import lax
from jax.experimental import pallas as pl
from jax.experimental.pallas import tpu as pltpu
from jax.sharding import PartitionSpec as P

HEADS = 8
K = 64
CROSS = 16
IN_MAX = 128
INNER = K - CROSS
MESH = pl.DeviceIdType.MESH
F32 = jnp.float32
BF = jnp.bfloat16


def mm(a, b):
    return lax.dot_general(a, b, (((1,), (0,)), ((), ())), preferred_element_type=F32)


def mt(a, b):
    return lax.dot_general(a, b, (((1,), (1,)), ((), ())), preferred_element_type=F32)


def iota(shape, dim):
    return lax.broadcasted_iota(jnp.int32, shape, dim).astype(F32)


def fdiv(x, c):
    return jnp.floor((x + 0.5) * (1.0 / c))


def onehot(a, b):
    return jnp.where(a == b, 1.0, 0.0).astype(BF)


def head_masks(width):
    lane = lax.broadcasted_iota(jnp.int32, (16, width), 1)
    size = width // HEADS
    return [
        jnp.where((lane >= h * size) & (lane < (h + 1) * size), 1.0, 0.0).astype(BF)[0:1]
        for h in range(HEADS)
    ]


def attend(proj, d_out, bias, masks):
    width = d_out.shape[1]
    size = width // HEADS
    scale = size ** -0.5
    queries = (proj[:, :width] * scale).astype(BF)
    keys = proj[:, width : 2 * width]
    values = proj[:, 2 * width :]
    keys_t = (keys.astype(F32) * scale).T.astype(BF)
    values_t = values.astype(F32).T.astype(BF)
    out_t, d_q_t = [], []
    d_k = d_v = None
    for pair in range(HEADS // 2):
        hs = (2 * pair, 2 * pair + 1)
        qb = jnp.concatenate([queries * masks[h] for h in hs], axis=0)
        gb = jnp.concatenate([d_out * masks[h] for h in hs], axis=0)
        scores = mt(keys, qb) + bias
        raised = jnp.exp(scores - jnp.max(scores, axis=0, keepdims=True))
        probs = raised * (1.0 / jnp.sum(raised, axis=0, keepdims=True))
        weights = probs.astype(BF)
        grad = mt(values, gb).astype(BF).astype(F32)
        total = jnp.sum(grad * probs, axis=0, keepdims=True)
        d_s = (probs * (grad - total)).astype(BF)
        part_v = mm(weights, gb)
        part_k = mm(d_s, qb)
        d_v = part_v if d_v is None else d_v + part_v
        d_k = part_k if d_k is None else d_k + part_k
        for i, h in enumerate(hs):
            rows = slice(h * size, (h + 1) * size)
            cols = slice(i * 128, (i + 1) * 128)
            out_t.append(mm(values_t[rows], weights[:, cols]))
            d_q_t.append(mm(keys_t[rows], d_s[:, cols]))
    out = jnp.concatenate(out_t, axis=0).T.astype(BF)
    d_q = jnp.concatenate(d_q_t, axis=0).T.astype(BF)
    return out, jnp.concatenate([d_q, d_k.astype(BF), d_v.astype(BF)], axis=1)


def kernel(
    n_arc, n_clu, group,
    deg_ref, feat_ref, cot_ref, wo_ref, wi_ref, wm_ref, order_ref,
    mixed_ref, grad_ref,
    packed, recv, ret, back, res, mix_part, grad_part, flat_row, flat_col,
    send_sem, recv_sem,
):
    rows, width = feat_ref.shape
    cities = rows // K
    per = INNER // n_arc
    slot = cities * per
    edge = cities * INNER
    me = lax.axis_index("arc")
    clu = lax.axis_index("clu")
    nxt, prv = lax.rem(clu + 1, n_clu), lax.rem(clu + n_clu - 1, n_clu)
    mef = me.astype(F32)

    barrier = pltpu.get_barrier_semaphore()
    for s in range(1, n_arc):
        pl.semaphore_signal(
            barrier, inc=1, device_id={"arc": lax.rem(me + s, n_arc)}, device_id_type=MESH
        )
    for other in (nxt, prv):
        pl.semaphore_signal(barrier, inc=1, device_id={"clu": other}, device_id_type=MESH)

    def copy(src, dst, s, leg, target):
        part = pl.ds(s * slot, slot) if s < n_arc else pl.ds(edge, cities * CROSS)
        index = leg * (n_arc + 1) + s
        return pltpu.make_async_remote_copy(
            src_ref=src.at[part],
            dst_ref=dst.at[part],
            send_sem=send_sem.at[index],
            recv_sem=recv_sem.at[index],
            device_id=target,
            device_id_type=MESH,
        )

    out_copies = [copy(packed, recv, n_arc, 0, {"clu": nxt})] + [
        copy(packed, recv, s, 0, {"arc": lax.rem(me + s, n_arc)}) for s in range(1, n_arc)
    ]
    home_copies = [copy(ret, back, n_arc, 1, {"clu": prv})] + [
        copy(ret, back, s, 1, {"arc": lax.rem(me + n_arc - s, n_arc)}) for s in range(1, n_arc)
    ]

    block = group * K
    g_slot = group * per
    g_edge = group * CROSS

    def place(src):
        city = fdiv(src, K)
        arc = src - city * K
        peer = fdiv(arc, per)
        j = arc - peer * per
        s = jnp.where(peer >= mef, peer - mef, peer - mef + n_arc)
        inner = s * g_slot + city * per + j
        return jnp.where(arc < INNER, inner, group * INNER + city * CROSS + (arc - INNER))

    wm = wm_ref[...]
    perm = onehot(place(iota((1, block), 1)), iota((block, block), 0))
    for g in range(cities // group):
        span = pl.ds(g * block, block)
        both = jnp.concatenate([feat_ref[span, :], cot_ref[span, :]], axis=1)
        moved = mm(perm, both).astype(BF)
        d_in = mt(moved[:, width:], wm[width:]).astype(BF)
        moved = jnp.concatenate([moved[:, :width], d_in], axis=1)
        for s in range(n_arc):
            packed[pl.ds(s * slot + g * g_slot, g_slot), :] = moved[s * g_slot : (s + 1) * g_slot]
        packed[pl.ds(edge + g * g_edge, g_edge), :] = moved[group * INNER :]

    pl.semaphore_wait(barrier, n_arc + 1)
    for c in out_copies:
        c.start()
    recv[pl.ds(0, slot), :] = packed[pl.ds(0, slot), :]

    where = order_ref[...].astype(F32)
    city = fdiv(where, INNER)
    arc = where - city * INNER
    peer = fdiv(arc, per)
    j = arc - peer * per
    s = jnp.where(mef >= peer, mef - peer, mef - peer + n_arc)
    where = jnp.where(where < edge, s * slot + city * per + j, where)
    pos = lax.broadcasted_iota(jnp.int32, (1, rows), 1)
    owner = jnp.full((1, rows), -1, jnp.int32)
    start = jnp.zeros((1, rows), jnp.int32)
    offset = jnp.int32(0)
    for t in range(cities):
        begun = pos >= offset
        owner = owner + jnp.where(begun, 1, 0)
        start = jnp.where(begun, offset, start)
        offset = offset + deg_ref[t]
    owner_f = owner.astype(F32)
    local_f = (pos - start).astype(F32)
    line = lax.broadcasted_iota(jnp.int32, (16, rows), 0)
    table = jnp.where(line == 0, owner_f, jnp.where(line == 1, local_f, 0.0)).astype(BF)
    for r in range(rows // 256):
        hits = onehot(where, iota((256, rows), 0) + r * 256)
        found = mt(table, hits)
        flat_row[:, r * 256 : (r + 1) * 256] = jnp.broadcast_to(
            found[0:1] * IN_MAX + found[1:2], (8, 256)
        )
        found = mt(hits, table)
        flat_col[r * 256 : (r + 1) * 256, :] = jnp.broadcast_to(
            found[:, 0:1] * IN_MAX + found[:, 1:2], (256, 128)
        )

    masks = head_masks(width)
    key_city = lax.broadcasted_iota(jnp.int32, (128, 256), 0) >= K
    lane = lax.broadcasted_iota(jnp.int32, (128, 256), 1)
    lane = jnp.where(lane >= 128, lane - 128, lane)
    pair_bias = jnp.where(key_city == (lane >= K), 0.0, -1e30)

    def out_step(c, carry):
        span = pl.ds(pl.multiple_of(c * 128, 128), 128)
        x = feat_ref[span, :]
        u = cot_ref[span, :]
        proj = mm(x, wo_ref[...]).astype(BF)
        d_out = mt(u, wm_ref[:width, :]).astype(BF)
        att, d_proj = attend(proj, d_out, pair_bias, masks)
        mix_part[span, :] = x.astype(F32) + mm(att, wm_ref[:width, :])
        grad_part[span, :] = u.astype(F32) + mt(d_proj, wo_ref[...])
        return carry

    pairs = rows // 128
    lax.fori_loop(0, pairs // 2, out_step, 0)
    for c in out_copies:
        c.wait()

    def in_step(t, carry):
        slots = (lax.broadcasted_iota(jnp.int32, (IN_MAX, rows), 0) + t * IN_MAX).astype(F32)
        pick = onehot(flat_row[0:1, :], slots)
        got = mm(pick, recv[...]).astype(BF)
        proj = mm(got[:, :width], wi_ref[...]).astype(BF)
        live = lax.broadcasted_iota(jnp.int32, (IN_MAX, 256), 0) < deg_ref[t]
        bias = jnp.where(live, 0.0, -1e30)
        att, d_proj = attend(proj, got[:, width:], bias, masks)
        span = pl.ds(pl.multiple_of(t * IN_MAX, IN_MAX), IN_MAX)
        res[span, :width] = att
        res[span, width:] = mt(d_proj, wi_ref[...]).astype(BF)
        return carry

    lax.fori_loop(0, cities, in_step, 0)

    slots = cities * IN_MAX

    def put_back(dst, begin, count):
        pick = onehot(flat_col[begin : begin + count, 0:1], iota((count, slots), 1))
        dst[begin : begin + count, :] = mm(pick, res[...]).astype(BF)

    put_back(ret, edge, cities * CROSS)
    home_copies[0].start()
    for s in range(1, n_arc):
        put_back(ret, s * slot, slot)
        home_copies[s].start()
    put_back(back, 0, slot)
    lax.fori_loop(pairs // 2, pairs, out_step, 0)
    for c in home_copies:
        c.wait()

    perm = onehot(place(iota((block, 1), 0)), iota((block, block), 1))
    for g in range(cities // group):
        moved = [back[pl.ds(s * slot + g * g_slot, g_slot), :] for s in range(n_arc)]
        moved.append(back[pl.ds(edge + g * g_edge, g_edge), :])
        home = mm(perm, jnp.concatenate(moved, axis=0))
        span = pl.ds(g * block, block)
        mixed_ref[span, :] = (
            mix_part[span, :] + mm(home[:, :width].astype(BF), wm[width:])
        ).astype(BF)
        grad_ref[span, :] = (grad_part[span, :] + home[:, width:]).astype(BF)


def body(features, cotangent, w_out_att, w_in_att, w_mix, in_degree, in_order):
    cities, arcs, width = features.shape[2:]
    rows = cities * arcs
    n_arc = lax.axis_size("arc")
    n_clu = lax.axis_size("clu")
    per = INNER // n_arc
    group = next(g for g in (4, 8, 16) if (g * per) % 16 == 0)
    vmem = pl.BlockSpec(memory_space=pltpu.VMEM)
    smem = pl.BlockSpec(memory_space=pltpu.SMEM)
    copies = 2 * (n_arc + 1)
    mixed, grad = pl.pallas_call(
        functools.partial(kernel, n_arc, n_clu, group),
        out_shape=[jax.ShapeDtypeStruct((rows, width), BF)] * 2,
        in_specs=[smem] + [vmem] * 6,
        out_specs=[vmem, vmem],
        scratch_shapes=[
            pltpu.VMEM((rows, 2 * width), BF),
            pltpu.VMEM((rows, 2 * width), BF),
            pltpu.VMEM((rows, 2 * width), BF),
            pltpu.VMEM((rows, 2 * width), BF),
            pltpu.VMEM((cities * IN_MAX, 2 * width), BF),
            pltpu.VMEM((rows, width), F32),
            pltpu.VMEM((rows, width), F32),
            pltpu.VMEM((8, rows), F32),
            pltpu.VMEM((rows, 128), F32),
            pltpu.SemaphoreType.DMA((copies,)),
            pltpu.SemaphoreType.DMA((copies,)),
        ],
        compiler_params=pltpu.CompilerParams(
            collective_id=0, has_side_effects=True, vmem_limit_bytes=48 * 1024 * 1024
        ),
    )(
        in_degree.reshape(cities),
        features.reshape(rows, width),
        cotangent.reshape(rows, width),
        w_out_att,
        w_in_att,
        w_mix,
        in_order.reshape(1, rows),
    )
    return mixed.reshape(features.shape), grad.reshape(features.shape)


def solution(mesh):
    in_specs = (
        P(("grp", "clu"), "arc", None, None, None),
        P(("grp", "clu"), "arc", None, None, None),
        P(),
        P(),
        P(),
        P(("grp", "clu"), "arc", None),
        P(("grp", "clu"), "arc", None),
    )
    out_specs = (
        P(("grp", "clu"), "arc", None, None, None),
        P(("grp", "clu"), "arc", None, None, None),
    )
    return jax.shard_map(body, mesh=mesh, in_specs=in_specs, out_specs=out_specs, check_vma=False)
```

time: 147 us -> 62.8 us (0.43)
  Pallas kernels: 0 us -> 55.2 us
  local copies, waits for them, and re-layouts: 61 us -> 6.6 us
  matrix products: 44 us -> 0 us
  starting transfers between devices: 21.4 us -> 0 us
  other arithmetic: 15.4 us -> 0 us
  waiting for transfers between devices: 3.14 us -> 0 us
    pallas_call x0 -> x1, Pallas kernels: none -> 55.2 us  [body(): pl.pallas_call(functools.partial(kernel, n_arc, n_clu, group), out_shape=...]
    gather x9 -> x0, local copies, waits for them, and re-layouts: 36.9 us -> none  [the longest x1 9.05 us: body(): tile_rows = grouped[slot_index]]
    dot_general x24 -> x0, matrix products: 36.5 us -> none  [the longest x9 20.9 us: attend(): jnp.einsum('bhqk,bkhd->bqhd', weights, values, preferred_element_type=jnp...]
    all_to_all x4 -> x0, starting transfers between devices: 14.9 us -> none  [the longest x2 7.58 us: to_targets(): lax.all_to_all(inside, 'arc', split_axis=1, concat_axis=1, tiled=True)]
    reduce_sum x7 -> x0, other arithmetic: 9.89 us -> none  [the longest x3 6.08 us: attend(): raised = jnp.exp(scores - highest)]
    sub x2 -> x0, matrix products: 7.47 us -> none  [attend(): raised = jnp.exp(scores - highest)]
    ppermute x4 -> x0, starting transfers between devices: 6.46 us -> none  [shifted(): return lax.ppermute(value, axis, pairs)]
    reshape x13 -> x0, local copies, waits for them, and re-layouts: 5.64 us -> none  [the longest x3 2.7 us: split_heads(): tensor.reshape(tensor.shape[:-1] + (HEADS, tensor.shape[-1] // HEADS))]
  transfers between devices with their start and end apart: 8 -> 0, of which waited for: 1 -> 0; matrix products, arithmetic and copies ran while one was open for 69% -> 0% of each run, Pallas kernels for 0% -> 0%
where the time goes in v1:
time: 62.8 us; the launch traced here: 62.5 us
  Pallas kernels  55.2 us (88%)
  local copies, waits for them, and re-layouts  6.6 us (11%)
  between operations  0.66 us (1%)
    pallas_call x1, Pallas kernels, body(): pl.pallas_call(functools.partial(kernel, n_arc, n_clu, group), out_shape=...  55.2 us
    unnamed x16, local copies, waits for them, and re-layouts  6.6 us

profile of v1, /device:TPU:0, one launch (start us, length us, event | category | flops | bytes accessed | tf_op | source)
XLA Modules:
  0.0 62.5 jit_solution(13368571854428570543)
XLA Ops:
  0.6 0.0 copy-start.5
  0.6 0.0 copy-start.6
  0.7 0.7 %copy-done.5 = s32[1,1,1024]{2,1,0:T(1,128)S(1)} copy-done((s32[1,1,1024]{2,1,0:T(1,128)S(1)}, s32[1,1,1024]{2,1,0:T(1,128)}, u32[]{:S(2)}) %copy-start.5) | copy-done | bytes 4120
  1.3 0.0 copy-done.6
  1.3 0.0 copy-start
  1.3 0.9 %copy-done = bf16[1,1,16,64,128]{4,3,2,1,0:T(8,128)(2,1)S(1)} copy-done((bf16[1,1,16,64,128]{4,3,2,1,0:T(8,128)(2,1)S(1)}, bf16[1,1,16,64,128]{4,3,2,1,0:T(8,128)(2,1)}, u32[]{:S(2)}) %copy-start) | copy-done | bytes 262168
  2.3 0.0 copy-start.1
  2.3 0.9 %copy-done.1 = bf16[1,1,16,64,128]{4,3,2,1,0:T(8,128)(2,1)S(1)} copy-done((bf16[1,1,16,64,128]{4,3,2,1,0:T(8,128)(2,1)S(1)}, bf16[1,1,16,64,128]{4,3,2,1,0:T(8,128)(2,1)}, u32[]{:S(2)}) %copy-start.1) | copy-done | bytes 262168
  3.2 0.0 copy-start.2
  3.2 0.9 %copy-done.2 = bf16[128,384]{1,0:T(8,128)(2,1)S(1)} copy-done((bf16[128,384]{1,0:T(8,128)(2,1)S(1)}, bf16[128,384]{1,0:T(8,128)(2,1)}, u32[]{:S(2)}) %copy-start.2) | copy-done | bytes 98328
  4.1 0.0 copy-start.3
  4.1 0.9 %copy-done.3 = bf16[128,384]{1,0:T(8,128)(2,1)S(1)} copy-done((bf16[128,384]{1,0:T(8,128)(2,1)S(1)}, bf16[128,384]{1,0:T(8,128)(2,1)}, u32[]{:S(2)}) %copy-start.3) | copy-done | bytes 98328
  5.0 0.0 copy-start.4
  5.0 0.8 %copy-done.4 = bf16[256,128]{1,0:T(8,128)(2,1)S(1)} copy-done((bf16[256,128]{1,0:T(8,128)(2,1)S(1)}, bf16[256,128]{1,0:T(8,128)(2,1)}, u32[]{:S(2)}) %copy-start.4) | copy-done | bytes 65560
  5.9 55.2 %shard_map.86 = (bf16[1024,128]{1,0:T(8,128)(2,1)S(1)}, bf16[1024,128]{1,0:T(8,128)(2,1)S(1)}) custom-call(s32[16]{0:T(128)S(1)} %bitcast.11, bf16[1024,128]{1,0:T(8,128)(2,1)S(1)} %bitcast.8, bf16[1024,128]{1,0:T(8,128)(2,1)S(1)} %bitcast.9, bf16[128,384]{1,0:T(8,128)(2,1)S(1)} %copy-done.2, bf16[128,384]{1,0:T(8,128)(2,1)S(1)} %copy-done.3, ...), custom_call_target="tpu_custom_call" | custom-call | tf_op jit(solution)/shard_map/pallas_call | solution.py:265
  61.1 0.7 %copy.11 = bf16[1,1,16,64,128]{4,3,2,1,0:T(8,128)(2,1)} copy(bf16[1,1,16,64,128]{4,3,2,1,0:T(8,128)(2,1)S(1)} %bitcast.7) | data formatting | bytes 524288
  61.8 0.7 %copy.12 = bf16[1,1,16,64,128]{4,3,2,1,0:T(8,128)(2,1)} copy(bf16[1,1,16,64,128]{4,3,2,1,0:T(8,128)(2,1)S(1)} %bitcast.6) | data formatting | bytes 524288
Async XLA Ops:
  0.6 0.7 %copy-start.5 = (s32[1,1,1024]{2,1,0:T(1,128)S(1)}, s32[1,1,1024]{2,1,0:T(1,128)}, u32[]{:S(2)}) copy-start(s32[1,1,1024]{2,1,0:T(1,128)} %param.13) | copy-start | bytes 12292
  0.6 0.7 %copy-start.6 = (s32[1,1,16]{2,1,0:T(1,128)S(1)}, s32[1,1,16]{2,1,0:T(1,128)}, u32[]{:S(2)}) copy-start(s32[1,1,16]{2,1,0:T(1,128)} %param.12) | copy-start | bytes 196
  1.3 1.0 %copy-start = (bf16[1,1,16,64,128]{4,3,2,1,0:T(8,128)(2,1)S(1)}, bf16[1,1,16,64,128]{4,3,2,1,0:T(8,128)(2,1)}, u32[]{:S(2)}) copy-start(bf16[1,1,16,64,128]{4,3,2,1,0:T(8,128)(2,1)} %param.7) | copy-start | bytes 786436
  2.3 0.9 %copy-start.1 = (bf16[1,1,16,64,128]{4,3,2,1,0:T(8,128)(2,1)S(1)}, bf16[1,1,16,64,128]{4,3,2,1,0:T(8,128)(2,1)}, u32[]{:S(2)}) copy-start(bf16[1,1,16,64,128]{4,3,2,1,0:T(8,128)(2,1)} %param.8) | copy-start | bytes 786436
  3.2 0.9 %copy-start.2 = (bf16[128,384]{1,0:T(8,128)(2,1)S(1)}, bf16[128,384]{1,0:T(8,128)(2,1)}, u32[]{:S(2)}) copy-start(bf16[128,384]{1,0:T(8,128)(2,1)} %wo_ref.1) | copy-start | bytes 294916
  4.1 0.9 %copy-start.3 = (bf16[128,384]{1,0:T(8,128)(2,1)S(1)}, bf16[128,384]{1,0:T(8,128)(2,1)}, u32[]{:S(2)}) copy-start(bf16[128,384]{1,0:T(8,128)(2,1)} %wi_ref.1) | copy-start | bytes 294916
  5.0 0.8 %copy-start.4 = (bf16[256,128]{1,0:T(8,128)(2,1)S(1)}, bf16[256,128]{1,0:T(8,128)(2,1)}, u32[]{:S(2)}) copy-start(bf16[256,128]{1,0:T(8,128)(2,1)} %wm_ref.1) | copy-start | bytes 196612

commit v2 on v1

--- a/solution.py
+++ b/solution.py
@@ -55,28 +55,25 @@
     values = proj[:, 2 * width :]
     keys_t = (keys.astype(F32) * scale).T.astype(BF)
     values_t = values.astype(F32).T.astype(BF)
+    qb = jnp.concatenate([queries * m for m in masks], axis=0)
+    gb = jnp.concatenate([d_out * m for m in masks], axis=0)
+    scores = mt(keys, qb) + jnp.concatenate([bias] * HEADS, axis=1)
+    raised = jnp.exp(scores - jnp.max(scores, axis=0, keepdims=True))
+    probs = raised * (1.0 / jnp.sum(raised, axis=0, keepdims=True))
+    weights = probs.astype(BF)
+    grad = mt(values, gb).astype(BF).astype(F32)
+    total = jnp.sum(grad * probs, axis=0, keepdims=True)
+    d_s = (probs * (grad - total)).astype(BF)
+    d_v = mm(weights, gb)
+    d_k = mm(d_s, qb)
     out_t, d_q_t = [], []
-    d_k = d_v = None
     for pair in range(HEADS // 2):
-        hs = (2 * pair, 2 * pair + 1)
-        qb = jnp.concatenate([queries * masks[h] for h in hs], axis=0)
-        gb = jnp.concatenate([d_out * masks[h] for h in hs], axis=0)
-        scores = mt(keys, qb) + bias
-        raised = jnp.exp(scores - jnp.max(scores, axis=0, keepdims=True))
-        probs = raised * (1.0 / jnp.sum(raised, axis=0, keepdims=True))
-        weights = probs.astype(BF)
-        grad = mt(values, gb).astype(BF).astype(F32)
-        total = jnp.sum(grad * probs, axis=0, keepdims=True)
-        d_s = (probs * (grad - total)).astype(BF)
-        part_v = mm(weights, gb)
-        part_k = mm(d_s, qb)
-        d_v = part_v if d_v is None else d_v + part_v
-        d_k = part_k if d_k is None else d_k + part_k
-        for i, h in enumerate(hs):
-            rows = slice(h * size, (h + 1) * size)
-            cols = slice(i * 128, (i + 1) * 128)
-            out_t.append(mm(values_t[rows], weights[:, cols]))
-            d_q_t.append(mm(keys_t[rows], d_s[:, cols]))
+        rows = slice(2 * pair * size, 2 * (pair + 1) * size)
+        cols = slice(pair * 256, (pair + 1) * 256)
+        part = mm(values_t[rows], weights[:, cols])
+        out_t += [part[:size, :128], part[size:, 128:]]
+        part = mm(keys_t[rows], d_s[:, cols])
+        d_q_t += [part[:size, :128], part[size:, 128:]]
     out = jnp.concatenate(out_t, axis=0).T.astype(BF)
     d_q = jnp.concatenate(d_q_t, axis=0).T.astype(BF)
     return out, jnp.concatenate([d_q, d_k.astype(BF), d_v.astype(BF)], axis=1)
@@ -84,11 +81,26 @@
 
 def kernel(
     n_arc, n_clu, group,
-    deg_ref, feat_ref, cot_ref, wo_ref, wi_ref, wm_ref, order_ref,
+    deg_ref, feat_hbm, cot_hbm, wo_hbm, wi_hbm, wm_hbm, order_ref,
     mixed_ref, grad_ref,
+    feat_ref, cot_ref, wo_ref, wi_ref, wm_ref,
     packed, recv, ret, back, res, mix_part, grad_part, flat_row, flat_col,
-    send_sem, recv_sem,
+    send_sem, recv_sem, load_sem,
 ):
+    loads = [
+        pltpu.make_async_copy(src, dst, load_sem.at[i])
+        for i, (src, dst) in enumerate(
+            [
+                (feat_hbm, feat_ref),
+                (cot_hbm, cot_ref),
+                (wm_hbm, wm_ref),
+                (wo_hbm, wo_ref),
+                (wi_hbm, wi_ref),
+            ]
+        )
+    ]
+    for c in loads:
+        c.start()
     rows, width = feat_ref.shape
     cities = rows // K
     per = INNER // n_arc
@@ -139,8 +151,10 @@
         inner = s * g_slot + city * per + j
         return jnp.where(arc < INNER, inner, group * INNER + city * CROSS + (arc - INNER))
 
+    perm = onehot(place(iota((1, block), 1)), iota((block, block), 0))
+    for c in loads:
+        c.wait()
     wm = wm_ref[...]
-    perm = onehot(place(iota((1, block), 1)), iota((block, block), 0))
     for g in range(cities // group):
         span = pl.ds(g * block, block)
         both = jnp.concatenate([feat_ref[span, :], cot_ref[span, :]], axis=1)
@@ -188,10 +202,10 @@
         )
 
     masks = head_masks(width)
-    key_city = lax.broadcasted_iota(jnp.int32, (128, 256), 0) >= K
-    lane = lax.broadcasted_iota(jnp.int32, (128, 256), 1)
-    lane = jnp.where(lane >= 128, lane - 128, lane)
-    pair_bias = jnp.where(key_city == (lane >= K), 0.0, -1e30)
+    key_row = lax.broadcasted_iota(jnp.int32, (128, 128), 0)
+    lane = lax.broadcasted_iota(jnp.int32, (128, 128), 1)
+    split = (key_row - K + 0.5).astype(F32) * (lane - K + 0.5).astype(F32)
+    pair_bias = jnp.where(split > 0, 0.0, -1e30)
 
     def out_step(c, carry):
         span = pl.ds(pl.multiple_of(c * 128, 128), 128)
@@ -205,7 +219,7 @@
         return carry
 
     pairs = rows // 128
-    lax.fori_loop(0, pairs // 2, out_step, 0)
+    lax.fori_loop(0, pairs // 2, out_step, 0, unroll=2)
     for c in out_copies:
         c.wait()
 
@@ -214,7 +228,7 @@
         pick = onehot(flat_row[0:1, :], slots)
         got = mm(pick, recv[...]).astype(BF)
         proj = mm(got[:, :width], wi_ref[...]).astype(BF)
-        live = lax.broadcasted_iota(jnp.int32, (IN_MAX, 256), 0) < deg_ref[t]
+        live = lax.broadcasted_iota(jnp.int32, (IN_MAX, IN_MAX), 0) < deg_ref[t]
         bias = jnp.where(live, 0.0, -1e30)
         att, d_proj = attend(proj, got[:, width:], bias, masks)
         span = pl.ds(pl.multiple_of(t * IN_MAX, IN_MAX), IN_MAX)
@@ -222,7 +236,7 @@
         res[span, width:] = mt(d_proj, wi_ref[...]).astype(BF)
         return carry
 
-    lax.fori_loop(0, cities, in_step, 0)
+    lax.fori_loop(0, cities, in_step, 0, unroll=2)
 
     slots = cities * IN_MAX
 
@@ -236,7 +250,7 @@
         put_back(ret, s * slot, slot)
         home_copies[s].start()
     put_back(back, 0, slot)
-    lax.fori_loop(pairs // 2, pairs, out_step, 0)
+    lax.fori_loop(pairs // 2, pairs, out_step, 0, unroll=2)
     for c in home_copies:
         c.wait()
 
@@ -265,9 +279,14 @@
     mixed, grad = pl.pallas_call(
         functools.partial(kernel, n_arc, n_clu, group),
         out_shape=[jax.ShapeDtypeStruct((rows, width), BF)] * 2,
-        in_specs=[smem] + [vmem] * 6,
+        in_specs=[smem] + [pl.BlockSpec(memory_space=pltpu.HBM)] * 5 + [vmem],
         out_specs=[vmem, vmem],
         scratch_shapes=[
+            pltpu.VMEM((rows, width), BF),
+            pltpu.VMEM((rows, width), BF),
+            pltpu.VMEM(w_out_att.shape, BF),
+            pltpu.VMEM(w_in_att.shape, BF),
+            pltpu.VMEM(w_mix.shape, BF),
             pltpu.VMEM((rows, 2 * width), BF),
             pltpu.VMEM((rows, 2 * width), BF),
             pltpu.VMEM((rows, 2 * width), BF),
@@ -279,6 +298,7 @@
             pltpu.VMEM((rows, 128), F32),
             pltpu.SemaphoreType.DMA((copies,)),
             pltpu.SemaphoreType.DMA((copies,)),
+            pltpu.SemaphoreType.DMA((5,)),
         ],
         compiler_params=pltpu.CompilerParams(
             collective_id=0, has_side_effects=True, vmem_limit_bytes=48 * 1024 * 1024

time: 62.8 us -> 47.3 us (0.75)
  Pallas kernels: 55.2 us -> 39.7 us
    pallas_call x1, Pallas kernels: 55.2 us -> 39.7 us  [body(): pl.pallas_call(functools.partial(kernel, n_arc, n_clu, group), out_shape=...]
where the time goes in v2:
time: 47.3 us; the launch traced here: 47 us
  Pallas kernels  39.7 us (84%)
  local copies, waits for them, and re-layouts  6.6 us (14%)
  between operations  0.66 us (1%)
    pallas_call x1, Pallas kernels, body(): pl.pallas_call(functools.partial(kernel, n_arc, n_clu, group), out_shape=...  39.7 us
    unnamed x16, local copies, waits for them, and re-layouts  6.6 us

profile of v2, /device:TPU:0, one launch (start us, length us, event | category | flops | bytes accessed | tf_op | source)
XLA Modules:
  0.0 47.0 jit_solution(13306797360297190781)
XLA Ops:
  0.6 0.0 copy-start.5
  0.6 0.0 copy-start.6
  0.7 0.7 %copy-done.5 = s32[1,1,1024]{2,1,0:T(1,128)S(1)} copy-done((s32[1,1,1024]{2,1,0:T(1,128)S(1)}, s32[1,1,1024]{2,1,0:T(1,128)}, u32[]{:S(2)}) %copy-start.5) | copy-done | bytes 4120
  1.3 0.0 copy-done.6
  1.3 0.0 copy-start
  1.3 0.9 %copy-done = bf16[1,1,16,64,128]{4,3,2,1,0:T(8,128)(2,1)S(1)} copy-done((bf16[1,1,16,64,128]{4,3,2,1,0:T(8,128)(2,1)S(1)}, bf16[1,1,16,64,128]{4,3,2,1,0:T(8,128)(2,1)}, u32[]{:S(2)}) %copy-start) | copy-done | bytes 262168
  2.3 0.0 copy-start.1
  2.3 0.9 %copy-done.1 = bf16[1,1,16,64,128]{4,3,2,1,0:T(8,128)(2,1)S(1)} copy-done((bf16[1,1,16,64,128]{4,3,2,1,0:T(8,128)(2,1)S(1)}, bf16[1,1,16,64,128]{4,3,2,1,0:T(8,128)(2,1)}, u32[]{:S(2)}) %copy-start.1) | copy-done | bytes 262168
  3.2 0.0 copy-start.2
  3.2 0.9 %copy-done.2 = bf16[128,384]{1,0:T(8,128)(2,1)S(1)} copy-done((bf16[128,384]{1,0:T(8,128)(2,1)S(1)}, bf16[128,384]{1,0:T(8,128)(2,1)}, u32[]{:S(2)}) %copy-start.2) | copy-done | bytes 98328
  4.1 0.0 copy-start.3
  4.1 0.9 %copy-done.3 = bf16[128,384]{1,0:T(8,128)(2,1)S(1)} copy-done((bf16[128,384]{1,0:T(8,128)(2,1)S(1)}, bf16[128,384]{1,0:T(8,128)(2,1)}, u32[]{:S(2)}) %copy-start.3) | copy-done | bytes 98328
  5.0 0.0 copy-start.4
  5.0 0.8 %copy-done.4 = bf16[256,128]{1,0:T(8,128)(2,1)S(1)} copy-done((bf16[256,128]{1,0:T(8,128)(2,1)S(1)}, bf16[256,128]{1,0:T(8,128)(2,1)}, u32[]{:S(2)}) %copy-start.4) | copy-done | bytes 65560
  5.9 39.7 %shard_map.86 = (bf16[1024,128]{1,0:T(8,128)(2,1)S(1)}, bf16[1024,128]{1,0:T(8,128)(2,1)S(1)}) custom-call(s32[16]{0:T(128)S(1)} %bitcast.11, bf16[1024,128]{1,0:T(8,128)(2,1)S(1)} %bitcast.8, bf16[1024,128]{1,0:T(8,128)(2,1)S(1)} %bitcast.9, bf16[128,384]{1,0:T(8,128)(2,1)S(1)} %copy-done.2, bf16[128,384]{1,0:T(8,128)(2,1)S(1)} %copy-done.3, ...), custom_call_target="tpu_custom_call" | custom-call | tf_op jit(solution)/shard_map/pallas_call | solution.py:279
  45.6 0.7 %copy.11 = bf16[1,1,16,64,128]{4,3,2,1,0:T(8,128)(2,1)} copy(bf16[1,1,16,64,128]{4,3,2,1,0:T(8,128)(2,1)S(1)} %bitcast.7) | data formatting | bytes 524288
  46.3 0.7 %copy.12 = bf16[1,1,16,64,128]{4,3,2,1,0:T(8,128)(2,1)} copy(bf16[1,1,16,64,128]{4,3,2,1,0:T(8,128)(2,1)S(1)} %bitcast.6) | data formatting | bytes 524288
Async XLA Ops:
  0.6 0.7 %copy-start.5 = (s32[1,1,1024]{2,1,0:T(1,128)S(1)}, s32[1,1,1024]{2,1,0:T(1,128)}, u32[]{:S(2)}) copy-start(s32[1,1,1024]{2,1,0:T(1,128)} %param.13) | copy-start | bytes 12292
  0.6 0.7 %copy-start.6 = (s32[1,1,16]{2,1,0:T(1,128)S(1)}, s32[1,1,16]{2,1,0:T(1,128)}, u32[]{:S(2)}) copy-start(s32[1,1,16]{2,1,0:T(1,128)} %param.12) | copy-start | bytes 196
  1.3 1.0 %copy-start = (bf16[1,1,16,64,128]{4,3,2,1,0:T(8,128)(2,1)S(1)}, bf16[1,1,16,64,128]{4,3,2,1,0:T(8,128)(2,1)}, u32[]{:S(2)}) copy-start(bf16[1,1,16,64,128]{4,3,2,1,0:T(8,128)(2,1)} %param.7) | copy-start | bytes 786436
  2.3 0.9 %copy-start.1 = (bf16[1,1,16,64,128]{4,3,2,1,0:T(8,128)(2,1)S(1)}, bf16[1,1,16,64,128]{4,3,2,1,0:T(8,128)(2,1)}, u32[]{:S(2)}) copy-start(bf16[1,1,16,64,128]{4,3,2,1,0:T(8,128)(2,1)} %param.8) | copy-start | bytes 786436
  3.2 0.9 %copy-start.2 = (bf16[128,384]{1,0:T(8,128)(2,1)S(1)}, bf16[128,384]{1,0:T(8,128)(2,1)}, u32[]{:S(2)}) copy-start(bf16[128,384]{1,0:T(8,128)(2,1)} %wo_hbm.1) | copy-start | bytes 294916
  4.1 0.9 %copy-start.3 = (bf16[128,384]{1,0:T(8,128)(2,1)S(1)}, bf16[128,384]{1,0:T(8,128)(2,1)}, u32[]{:S(2)}) copy-start(bf16[128,384]{1,0:T(8,128)(2,1)} %wi_hbm.1) | copy-start | bytes 294916
  5.0 0.8 %copy-start.4 = (bf16[256,128]{1,0:T(8,128)(2,1)S(1)}, bf16[256,128]{1,0:T(8,128)(2,1)}, u32[]{:S(2)}) copy-start(bf16[256,128]{1,0:T(8,128)(2,1)} %wm_hbm.1) | copy-start | bytes 196612

commit v3 on v2

--- a/solution.py
+++ b/solution.py
@@ -83,7 +83,7 @@
     n_arc, n_clu, group,
     deg_ref, feat_hbm, cot_hbm, wo_hbm, wi_hbm, wm_hbm, order_ref,
     mixed_ref, grad_ref,
-    feat_ref, cot_ref, wo_ref, wi_ref, wm_ref,
+    feat_ref, cot_ref, wo_ref, wi_ref, wm_ref, proj_in, d_got,
     packed, recv, ret, back, res, mix_part, grad_part, flat_row, flat_col,
     send_sem, recv_sem, load_sem,
 ):
@@ -223,20 +223,32 @@
     for c in out_copies:
         c.wait()
 
-    def in_step(t, carry):
-        slots = (lax.broadcasted_iota(jnp.int32, (IN_MAX, rows), 0) + t * IN_MAX).astype(F32)
+    def gather_step(b, carry):
+        slots = (lax.broadcasted_iota(jnp.int32, (512, rows), 0) + b * 512).astype(F32)
         pick = onehot(flat_row[0:1, :], slots)
         got = mm(pick, recv[...]).astype(BF)
-        proj = mm(got[:, :width], wi_ref[...]).astype(BF)
+        span = pl.ds(pl.multiple_of(b * 512, 512), 512)
+        proj_in[span, :] = mm(got[:, :width], wi_ref[...]).astype(BF)
+        d_got[span, :] = got[:, width:]
+        return carry
+
+    def in_step(t, carry):
         live = lax.broadcasted_iota(jnp.int32, (IN_MAX, IN_MAX), 0) < deg_ref[t]
         bias = jnp.where(live, 0.0, -1e30)
-        att, d_proj = attend(proj, got[:, width:], bias, masks)
         span = pl.ds(pl.multiple_of(t * IN_MAX, IN_MAX), IN_MAX)
+        att, d_proj = attend(proj_in[span, :], d_got[span, :], bias, masks)
         res[span, :width] = att
-        res[span, width:] = mt(d_proj, wi_ref[...]).astype(BF)
+        proj_in[span, :] = d_proj
         return carry
 
+    def pull_step(b, carry):
+        span = pl.ds(pl.multiple_of(b * 512, 512), 512)
+        res[span, width:] = mt(proj_in[span, :], wi_ref[...]).astype(BF)
+        return carry
+
+    lax.fori_loop(0, cities * IN_MAX // 512, gather_step, 0)
     lax.fori_loop(0, cities, in_step, 0, unroll=2)
+    lax.fori_loop(0, cities * IN_MAX // 512, pull_step, 0)
 
     slots = cities * IN_MAX
 
@@ -287,6 +299,8 @@
             pltpu.VMEM(w_out_att.shape, BF),
             pltpu.VMEM(w_in_att.shape, BF),
             pltpu.VMEM(w_mix.shape, BF),
+            pltpu.VMEM((cities * IN_MAX, 3 * width), BF),
+            pltpu.VMEM((cities * IN_MAX, width), BF),
             pltpu.VMEM((rows, 2 * width), BF),
             pltpu.VMEM((rows, 2 * width), BF),
             pltpu.VMEM((rows, 2 * width), BF),
@@ -301,7 +315,7 @@
             pltpu.SemaphoreType.DMA((5,)),
         ],
         compiler_params=pltpu.CompilerParams(
-            collective_id=0, has_side_effects=True, vmem_limit_bytes=48 * 1024 * 1024
+            collective_id=0, has_side_effects=True, vmem_limit_bytes=63*1024*1024
         ),
     )(
         in_degree.reshape(cities),

time: 47.3 us -> 40.9 us (0.86)
  local copies, waits for them, and re-layouts: 6.6 us -> 2.42 us
  Pallas kernels: 39.7 us -> 37.6 us
    unnamed x16 -> x4, local copies, waits for them, and re-layouts: 6.6 us -> 2.42 us
    pallas_call x1, Pallas kernels: 39.7 us -> 37.6 us  [body(): pl.pallas_call(functools.partial(kernel, n_arc, n_clu, group), out_shape=...]
where the time goes in v3:
time: 40.9 us; the launch traced here: 40.7 us
  Pallas kernels  37.6 us (92%)
  local copies, waits for them, and re-layouts  2.42 us (6%)
  between operations  0.65 us (2%)
    pallas_call x1, Pallas kernels, body(): pl.pallas_call(functools.partial(kernel, n_arc, n_clu, group), out_shape=...  37.6 us
    unnamed x4, local copies, waits for them, and re-layouts  2.42 us

profile of v3, /device:TPU:0, one launch (start us, length us, event | category | flops | bytes accessed | tf_op | source)
XLA Modules:
  0.0 40.7 jit_solution(11485687684195111156)
XLA Ops:
  0.6 37.6 %shard_map.86 = (bf16[1024,128]{1,0:T(8,128)(2,1)}, bf16[1024,128]{1,0:T(8,128)(2,1)}) custom-call(s32[16]{0:T(128)} %bitcast.11, bf16[1024,128]{1,0:T(8,128)(2,1)} %bitcast.8, bf16[1024,128]{1,0:T(8,128)(2,1)} %bitcast.9, bf16[128,384]{1,0:T(8,128)(2,1)} %wo_hbm.1, bf16[128,384]{1,0:T(8,128)(2,1)} %wi_hbm.1, bf16[256,128]{1,0:T(8,128)(2,1)} %wm_hbm.1, ...), custom_call_target="tpu_custom_call" | custom-call | tf_op jit(solution)/shard_map/pallas_call | solution.py:291
  38.3 0.0 copy-start
  38.3 1.7 %copy.11 = bf16[1,1,16,64,128]{4,3,2,1,0:T(8,128)(2,1)} copy(bf16[1,1,16,64,128]{4,3,2,1,0:T(8,128)(2,1)} %bitcast.7) | data formatting | bytes 524288
  40.0 0.0 copy-done
  40.0 0.7 %copy.12 = bf16[1,1,16,64,128]{4,3,2,1,0:T(8,128)(2,1)} copy(bf16[1,1,16,64,128]{4,3,2,1,0:T(8,128)(2,1)S(1)} %bitcast.6) | data formatting | bytes 524288
Async XLA Ops:
  38.3 1.7 %copy-start = (bf16[1024,128]{1,0:T(8,128)(2,1)S(1)}, bf16[1024,128]{1,0:T(8,128)(2,1)}, u32[]{:S(2)}) copy-start(bf16[1024,128]{1,0:T(8,128)(2,1)} %get-tuple-element.5) | copy-start | bytes 786436

commit v4 on v3

--- a/solution.py
+++ b/solution.py
@@ -131,9 +131,10 @@
             device_id_type=MESH,
         )
 
-    out_copies = [copy(packed, recv, n_arc, 0, {"clu": nxt})] + [
-        copy(packed, recv, s, 0, {"arc": lax.rem(me + s, n_arc)}) for s in range(1, n_arc)
-    ]
+    far = sorted(range(1, n_arc), key=lambda s: abs(2 * s - n_arc))
+    out_copies = [
+        copy(packed, recv, s, 0, {"arc": lax.rem(me + s, n_arc)}) for s in far
+    ] + [copy(packed, recv, n_arc, 0, {"clu": nxt})]
     home_copies = [copy(ret, back, n_arc, 1, {"clu": prv})] + [
         copy(ret, back, s, 1, {"arc": lax.rem(me + n_arc - s, n_arc)}) for s in range(1, n_arc)
     ]
@@ -247,7 +248,7 @@
         return carry
 
     lax.fori_loop(0, cities * IN_MAX // 512, gather_step, 0)
-    lax.fori_loop(0, cities, in_step, 0, unroll=2)
+    lax.fori_loop(0, cities, in_step, 0, unroll=4)
     lax.fori_loop(0, cities * IN_MAX // 512, pull_step, 0)
 
     slots = cities * IN_MAX

time: 40.9 us -> 41.1 us (level)
  no operation moved by 1% of the time
where the time goes in v4:
time: 41.1 us; the launch traced here: 40.9 us
  Pallas kernels  37.8 us (92%)
  local copies, waits for them, and re-layouts  2.42 us (6%)
  between operations  0.65 us (2%)
    pallas_call x1, Pallas kernels, body(): pl.pallas_call(functools.partial(kernel, n_arc, n_clu, group), out_shape=...  37.8 us
    unnamed x4, local copies, waits for them, and re-layouts  2.42 us

profile of v4, /device:TPU:0, one launch (start us, length us, event | category | flops | bytes accessed | tf_op | source)
XLA Modules:
  0.0 40.9 jit_solution(26863589491975460)
XLA Ops:
  0.6 37.8 %shard_map.86 = (bf16[1024,128]{1,0:T(8,128)(2,1)}, bf16[1024,128]{1,0:T(8,128)(2,1)}) custom-call(s32[16]{0:T(128)} %bitcast.11, bf16[1024,128]{1,0:T(8,128)(2,1)} %bitcast.8, bf16[1024,128]{1,0:T(8,128)(2,1)} %bitcast.9, bf16[128,384]{1,0:T(8,128)(2,1)} %wo_hbm.1, bf16[128,384]{1,0:T(8,128)(2,1)} %wi_hbm.1, bf16[256,128]{1,0:T(8,128)(2,1)} %wm_hbm.1, ...), custom_call_target="tpu_custom_call" | custom-call | tf_op jit(solution)/shard_map/pallas_call | solution.py:292
  38.4 0.0 copy-start
  38.4 1.7 %copy.11 = bf16[1,1,16,64,128]{4,3,2,1,0:T(8,128)(2,1)} copy(bf16[1,1,16,64,128]{4,3,2,1,0:T(8,128)(2,1)} %bitcast.7) | data formatting | bytes 524288
  40.2 0.0 copy-done
  40.2 0.7 %copy.12 = bf16[1,1,16,64,128]{4,3,2,1,0:T(8,128)(2,1)} copy(bf16[1,1,16,64,128]{4,3,2,1,0:T(8,128)(2,1)S(1)} %bitcast.6) | data formatting | bytes 524288
Async XLA Ops:
  38.4 1.7 %copy-start = (bf16[1024,128]{1,0:T(8,128)(2,1)S(1)}, bf16[1024,128]{1,0:T(8,128)(2,1)}, u32[]{:S(2)}) copy-start(bf16[1024,128]{1,0:T(8,128)(2,1)} %get-tuple-element.5) | copy-start | bytes 786436
